TPU v7x, 128 devices: a whole 4x4x4 slice. The times are simulated.
128 devices in a mesh: train: 16 (over y_hi, x, core), query: 8 (over y_lo, z).
Axes of the slice: x: 4, y: 4 (y_hi: 2, y_lo: 2; y = y_hi * 2 + y_lo), z: 4, core: 2. Of those that a mesh axis runs over, the one named last changes fastest.
Arguments:
- train_grads: bfloat16 [262144, 2048], P(('train', 'query')), may hold values from -128 to 128
- query_grads: bfloat16 [512, 2048], P(('train', 'query')), may hold values from -6 to 6
Outputs:
- scores: float32 [262144, 512], P(('train', 'query'))
- solved: float32 [512, 2048], P(('train', 'query'))
All inputs are finite; a program needn't handle non-finite values.
Results may differ from a plain program's by a relative error of at most 0.0013.
The roundings to bfloat16 on the way count: a program that leaves them out, or rounds other values in their place, can miss the bound.
Values may be sent and summed in bfloat16 or wider, within the bound.
A program may use at most 64 MiB of HBM per device.

v0:
```python
import jax
import jax.numpy as jnp
from jax import lax
from jax.sharding import PartitionSpec as P

ITERS = 2


def body(train_grads, query_grads):
    width = train_grads.shape[1]
    own_sum = jnp.sum(jnp.square(train_grads.astype(jnp.float32)))
    total = lax.psum(own_sum, ("train", "query"))
    coef = width / (8.0 * total)

    def against(piece):
        return lax.dot_general(
            train_grads, piece, (((1,), (1,)), ((), ())), preferred_element_type=jnp.float32
        )

    def project(state):
        low_state = state.astype(jnp.bfloat16)
        return against(lax.all_gather(low_state, ("train", "query"), axis=0, tiled=True))

    query = query_grads.astype(jnp.float32)
    solved = query
    for step in range(ITERS):
        inner = project(solved).astype(jnp.bfloat16)
        solved = (
            query
            + 0.99 * solved
            - coef
            * lax.psum_scatter(
                lax.dot_general(
                    inner, train_grads, (((0,), (0,)), ((), ())), preferred_element_type=jnp.float32
                ),
                ("train", "query"),
                scatter_dimension=0,
                tiled=True,
            )
        )
    scores = project(solved) * (1.0 / width**0.5)
    return (scores, solved)


def solution(mesh):
    placed = (P(("train", "query"), None), P(("train", "query"), None))
    return jax.shard_map(
        body,
        mesh=mesh,
        in_specs=placed,
        out_specs=(P(("train", "query"), None), P(("train", "query"), None)),
        check_vma=False,
    )
```

profile of v0, /device:TPU:1, one launch (start us, length us, event | category | flops | bytes accessed | tf_op | source)
XLA Modules:
  0.0 1289.8 jit_solution(17201918331867355236)
XLA Ops:
  7.2 0.0 all-gather.7.cloned.1.call-start
  7.2 0.7 all-gather.7.cloned.1.call-update
  7.9 0.0 all-reduce.5.cloned.1.call-start
  7.9 306.5 %all-gather.7.cloned.1.call-done = bf16[128,4,2048]{2,1,0:T(4,128)(2,1)} async-done(((bf16[1,4,2048]{2,1,0:T(4,128)(2,1)}), bf16[128,4,2048]{2,1,0:T(4,128)(2,1)}) %all-gather.7.cloned.1.call-update) | async-done | bytes 2097168 | tf_op jit(solution)/shard_map/all_gather | solution.py:22
  314.4 2.5 reshape.5
  317.0 16.7 %fusion.4 = f32[512,2048]{1,0:T(8,128)} fusion(bf16[2048,2048]{1,0:T(8,128)(2,1)} %param.2, bf16[512,2048]{1,0:T(8,128)(2,1)S(1)} %reshape.5), kind=kOutput, calls=%fused_computation.13 | convolution fusion | flops 8590983168 | bytes 14680064 | tf_op jit(solution)/shard_map/dot_general | solution.py:33
  333.7 0.0 all-reduce.5.cloned.1.call-update
  333.7 0.0 copy-start
  333.7 0.0 all-gather.9.cloned.1.call-start
  333.8 8.3 multiply_reduce_fusion
  342.1 66.3 %psum.7 = f32[]{:T(128)} all-reduce(f32[]{:T(128)} %multiply_reduce_fusion), channel_id=1, replica_groups=mesh['train'=16,'query'=8] {'train','query'}, use_global_device_ids=true, to_apply=%region_1.0 | all-reduce | flops 1 | bytes 8 | tf_op jit(solution)/shard_map/psum | solution.py:12
  409.0 79.4 %all-reduce.5.cloned.1.call-done = f32[512,2048]{1,0:T(8,128)} async-done(((f32[512,2048]{1,0:T(8,128)}), f32[512,2048]{1,0:T(8,128)}) %all-reduce.5.cloned.1.call-update) | async-done | bytes 4194320
  488.4 0.0 copy-done
  488.4 1.5 convert_bitcast_fusion.1
  489.9 0.0 all-gather.9.cloned.1.call-update
  489.9 0.0 all-reduce.7.cloned.1.call-start
  490.0 300.6 %all-gather.9.cloned.1.call-done = bf16[128,4,2048]{2,1,0:T(4,128)(2,1)} async-done(((bf16[1,4,2048]{2,1,0:T(4,128)(2,1)}), bf16[128,4,2048]{2,1,0:T(4,128)(2,1)}) %all-gather.9.cloned.1.call-update) | async-done | bytes 2097168 | tf_op jit(solution)/shard_map/all_gather | solution.py:22
  790.6 2.5 reshape.7
  793.1 16.6 %fusion = f32[512,2048]{1,0:T(8,128)} fusion(bf16[2048,2048]{1,0:T(8,128)(2,1)} %param.2, bf16[512,2048]{1,0:T(8,128)(2,1)S(1)} %reshape.7), kind=kOutput, calls=%fused_computation.4 | convolution fusion | flops 8590983168 | bytes 14680064 | tf_op jit(solution)/shard_map/dot_general | solution.py:33
  809.7 0.0 all-reduce.7.cloned.1.call-update
  809.8 0.0 all-gather.11.cloned.1.call-start
  809.8 154.2 %all-reduce.7.cloned.1.call-done = f32[512,2048]{1,0:T(8,128)} async-done(((f32[512,2048]{1,0:T(8,128)}), f32[512,2048]{1,0:T(8,128)}) %all-reduce.7.cloned.1.call-update) | async-done | bytes 4194320
  964.0 1.5 convert_bitcast_fusion
  965.5 0.0 all-gather.11.cloned.1.call-update
  965.6 300.4 %all-gather.11.cloned.1.call-done = bf16[128,4,2048]{2,1,0:T(4,128)(2,1)} async-done(((bf16[1,4,2048]{2,1,0:T(4,128)(2,1)}), bf16[128,4,2048]{2,1,0:T(4,128)(2,1)}) %all-gather.11.cloned.1.call-update) | async-done | bytes 2097168 | tf_op jit(solution)/shard_map/all_gather | solution.py:22
  1266.0 2.5 reshape.9
  1268.5 9.4 multiply_bitcast_fusion
  1278.0 5.3 copy.5
Async XLA Ops:
  7.2 307.3 %all-gather.7.cloned.1.call-start = ((), (), s32[]{:S(2)}) async-start(), calls=%async_computation | async-start | bytes 2113536 | tf_op jit(solution)/shard_map/all_gather | solution.py:22
  7.9 480.5 %all-reduce.5.cloned.1.call-start = ((), (), s32[]{:S(2)}) async-start(), calls=%async_computation.3 | async-start | bytes 8388608
  333.7 154.7 %copy-start = (bf16[4,2048]{1,0:T(4,128)(2,1)S(1)}, bf16[4,2048]{1,0:T(4,128)(2,1)}, u32[]{:S(2)}) copy-start(bf16[4,2048]{1,0:T(4,128)(2,1)} %param.3) | copy-start | bytes 49156
  333.7 456.8 %all-gather.9.cloned.1.call-start = ((), (), s32[]{:S(2)}) async-start(), calls=%async_computation.1 | async-start | bytes 2113536 | tf_op jit(solution)/shard_map/all_gather | solution.py:22
  489.9 474.1 %all-reduce.7.cloned.1.call-start = ((), (), s32[]{:S(2)}) async-start(), calls=%async_computation.4 | async-start | bytes 8388608
  809.8 456.2 %all-gather.11.cloned.1.call-start = ((), (), s32[]{:S(2)}) async-start(), calls=%async_computation.2 | async-start | bytes 2113536 | tf_op jit(solution)/shard_map/all_gather | solution.py:22
Sparse Core Ops, SparseCore 0:
  9.7 304.6 all-gather.6
  333.8 154.5 all-reduce.4
  490.7 299.8 all-gather.8
  809.9 154.0 all-reduce.6
  966.1 299.8 all-gather.10
where the time goes:
time: 1290 us
  waiting for transfers between devices  1140 us (88%)
  blocking collectives  66.3 us (5%)
  matrix products  42.8 us (3%)
  between operations  14.5 us (1%)
  local copies, waits for them, and re-layouts  12.9 us (1%)
    all_gather x3, waiting for transfers between devices, project(): lax.all_gather(low_state, ('train', 'query'), axis=0, tiled=True)  908 us
    unnamed x7, waiting for transfers between devices  234 us
    psum x1, blocking collectives, body(): total = lax.psum(own_sum, ('train', 'query'))  66.3 us
    dot_general x2, matrix products, body(): lax.dot_general(inner, train_grads, (((0,), (0,)), ((), ())), preferred_e...  33.4 us
  transfers between devices with their start and end apart: 5, of which 5 were waited for; matrix products, arithmetic and copies ran while one was open for 1% of the time, Pallas kernels for 0%

commit v1 on v0

v1 whole, which is shorter than its diff:
```python
import functools

import jax
import jax.numpy as jnp
from jax import lax
from jax.experimental import pallas as pl
from jax.experimental.pallas import tpu as pltpu
from jax.sharding import PartitionSpec as P

ITERS = 2
MESH = pl.DeviceIdType.MESH
F32, BF16 = jnp.float32, jnp.bfloat16
ORDER = (0, 1, 3, 2)
TILE = 512


def div(a, b):
    return lax.div(a, jnp.int32(b))


def rem(a, b):
    return lax.rem(a, jnp.int32(b))


def nt(a, b):
    return lax.dot_general(a, b, (((1,), (1,)), ((), ())), preferred_element_type=F32)


def nn(a, b):
    return lax.dot_general(a, b, (((1,), (0,)), ((), ())), preferred_element_type=F32)


def wait_for(ref, sem):
    pltpu.make_async_copy(ref, ref, sem).wait()


def kernel(
    grads_ref, query_ref, scores_ref, solved_ref,
    grads, low, low_all, acc, inner, outgoing, arrived, scores,
    row_out, row_in, query, state, squares, square_out, squares_in,
    grads_sems, row_sems, gather_send, gather_recv, pair_send, pair_recv,
    reduce_send, reduce_recv, square_sems, out_sem,
):
    rows, width = grads_ref.shape
    quarter = width // 4
    half = low.shape[2]
    train, along = lax.axis_index("train"), lax.axis_index("query")
    core, x, y_hi = rem(train, 2), rem(div(train, 2), 4), div(train, 8)
    y_lo, z = div(along, 4), rem(along, 4)
    y = y_hi * 2 + y_lo

    def group_of(px, py):
        return (div(py, 2) * 4 + px) * 2 + rem(py, 2)

    def peer(at, dz):
        px, py, pz = rem(x + div(at, 4), 4), rem(y + rem(at, 4), 4), rem(z + dz, 4)
        return (div(py, 2) * 8 + px * 2 + core, rem(py, 2) * 4 + pz), group_of(px, py)

    blocks = arrived.at[0, pl.ds(1, 63)]
    sibling = (train + 1 - 2 * core, along)
    mine = group_of(x, y)
    mine_at = pl.multiple_of(mine * 16, 16)
    all_at = pl.multiple_of(div(mine, 2) * 64 + core * 32 + rem(mine, 2) * 16, 16)

    def remote(src, dst, send, recv, to):
        return pltpu.make_async_remote_copy(
            src_ref=src, dst_ref=dst, send_sem=send, recv_sem=recv, device_id=to, device_id_type=MESH
        )

    own_load = pltpu.make_async_copy(grads_ref, grads.at[pl.ds(0, rows)], grads_sems.at[0])
    own_load.start()

    barrier = pltpu.get_barrier_semaphore()
    pl.semaphore_signal(barrier, inc=1, device_id=sibling, device_id_type=MESH)

    def greet(n, carry):
        to, _ = peer(rem(n, 16), div(n, 16))
        pl.semaphore_signal(barrier, inc=1, device_id=to, device_id_type=MESH)
        return carry

    lax.fori_loop(1, 64, greet, 0)
    row_out[...] = jnp.zeros_like(row_out)
    for p in range(4):
        row_out[p, 0:4, :] = query_ref[:, p * quarter : (p + 1) * quarter].astype(F32)
    pl.semaphore_wait(barrier, 64)

    def exchange_rows(sems):
        for dz in range(1, 4):
            to, _ = peer(jnp.int32(0), dz)
            remote(row_out.at[rem(z + dz, 4)], row_in.at[z], sems.at[0], sems.at[1], to).start()
        row_in[z] = row_out[z]

    exchange_rows(row_sems.at[0])
    pair_load = remote(grads_ref, grads.at[pl.ds(rows, rows)], grads_sems.at[1], grads_sems.at[2], sibling)
    pair_load.start()
    wait_for(row_in.at[pl.ds(0, 3)], row_sems.at[0, 1])
    for p in range(4):
        query[p * 4 : p * 4 + 4, :] = row_in[p, 0:4, :]
    state[...] = query[...]
    wait_for(row_out.at[pl.ds(0, 3)], row_sems.at[0, 0])

    def gather(step, buffer, at):
        buffer[z, pl.ds(at, 16), :] = state[...].astype(BF16)
        block = buffer.at[z, pl.ds(at, 16)]
        for dz in ORDER:
            def send(n, carry, dz=dz):
                to, _ = peer(n, dz)
                remote(block, block, gather_send.at[step], gather_recv.at[step, dz], to).start()
                return carry

            lax.fori_loop(1 if dz == 0 else 0, 16, send, 0)

    def await_group(step, dz):
        taken = low.at[0, 0]
        wait_for(taken.at[pl.ds(0, 240)] if dz == 0 else taken, gather_recv.at[step, dz])

    def project(step, k, first, last):
        p = rem(z + 4 - ORDER[k], 4)
        columns = pl.ds(pl.multiple_of(p * quarter, quarter), quarter)

        @pl.loop(first // TILE, last // TILE)
        def _(i):
            here = pl.ds(pl.multiple_of(i * TILE, TILE), TILE)
            part = nt(low[step, p], grads[here, columns])
            if k == 0:
                acc[:, here] = part
            elif k < 3:
                acc[:, here] += part
            else:
                inner[:, here] = (acc[:, here] + part).astype(BF16)

    def reduce(step):
        @pl.loop(0, 4)
        def _(j):
            dz = rem(j + 1, 4)
            p = rem(z + dz, 4)
            columns = pl.ds(pl.multiple_of(p * quarter, quarter), quarter)
            outgoing[j] = nn(inner[...], grads[:, columns]).astype(BF16)

            def send(n, carry):
                @pl.when(n + dz > 0)
                def _():
                    to, group = peer(n, dz)
                    remote(
                        outgoing.at[j, pl.ds(pl.multiple_of(group * 16, 16), 16)],
                        arrived.at[step, dz * 16 + n],
                        reduce_send.at[step],
                        reduce_recv.at[step, dz],
                        to,
                    ).start()

                return carry

            lax.fori_loop(0, 16, send, 0)

        def add(first, last, total):
            return lax.fori_loop(first, last, lambda n, t: t + arrived[step, n].astype(F32), total)

        total = outgoing[3, pl.ds(mine_at, 16), :].astype(F32)
        for dz in (1, 2, 3):
            wait_for(arrived.at[step, pl.ds(dz * 16, 16)], reduce_recv.at[step, dz])
            total = add(dz * 16, dz * 16 + 16, total)
        wait_for(arrived.at[step, pl.ds(1, 15)], reduce_recv.at[step, 0])
        return add(1, 16, total)

    gather(0, low.at[0], mine_at)

    own_load.wait()

    def square(i, total):
        strip = pl.ds(pl.multiple_of(i * 256, 256), 256)
        part = jnp.zeros((256, 128), F32)
        for j in range(width // 128):
            value = grads[strip, j * 128 : (j + 1) * 128].astype(F32)
            part = part + value * value
        return total + jnp.sum(part.reshape(32, 8, 128), axis=0)

    own = lax.fori_loop(0, rows // 256, square, jnp.zeros((8, 128), F32))
    square_out[0] = jnp.sum(own, axis=0, keepdims=True)
    to_sibling = remote(square_out.at[0], square_out.at[1], square_sems.at[0], square_sems.at[1], sibling)
    to_sibling.start()
    to_sibling.wait()
    squares_in[0] = square_out[0] + square_out[1]

    def send_squares(n, carry):
        to, _ = peer(rem(n, 16), div(n, 16))
        remote(squares_in.at[0], squares_in.at[n], square_sems.at[2], square_sems.at[3], to).start()
        return carry

    lax.fori_loop(1, 64, send_squares, 0)

    for k in range(4):
        await_group(0, ORDER[k])
        project(0, k, 0, rows)
    pair_load.wait_recv()
    for k in range(4):
        project(0, k, rows, 2 * rows)

    coef = None
    for step in range(ITERS):
        if step > 0:
            for k in range(4):
                await_group(step, ORDER[k])
                project(step, k, 0, 2 * rows)
            wait_for(blocks, reduce_send.at[step - 1])
        curve = reduce(step)
        if step == 0:
            wait_for(squares_in.at[pl.ds(1, 63)], square_sems.at[3])
            coef = width / (8.0 * jnp.sum(squares_in[...]))
        state[...] = query[...] + 0.99 * state[...] - coef * curve
        if step < ITERS - 1:
            gather(step + 1, low.at[step + 1], mine_at)
        else:
            gather(step + 1, low_all, all_at)

    for p in range(4):
        row_out[p, 0:4, :] = state[p * 4 : p * 4 + 4, :]
    exchange_rows(row_sems.at[1])

    def strip_of(p, m):
        return low_all.at[p, pl.ds(pl.multiple_of(m * 64 + core * 32, 32), 32)]

    def score(k):
        p = rem(z + 4 - ORDER[k], 4)
        columns = pl.ds(pl.multiple_of(p * quarter, quarter), quarter)

        @pl.loop(0, rows // TILE)
        def _(i):
            here = pl.ds(pl.multiple_of(i * TILE, TILE), TILE)
            part = nt(grads[here, columns], low_all[p])
            if k == 0:
                scores[here, :] = part
            elif k < 3:
                scores[here, :] += part
            else:
                scores[here, :] = (scores[here, :] + part) * (1.0 / width**0.5)
                pltpu.make_async_copy(scores.at[here], scores_ref.at[here], out_sem).start()

    for k in range(5):
        if k < 4:
            await_group(ITERS, ORDER[k])
            p = rem(z + 4 - ORDER[k], 4)

            def pass_on(m, carry, p=p, k=k):
                strip = strip_of(p, m)
                remote(strip, strip, pair_send, pair_recv.at[k], sibling).start()
                return carry

            lax.fori_loop(0, 8, pass_on, 0)
        if k > 0:
            wait_for(low.at[0, 0], pair_recv.at[k - 1])
            score(k - 1)

    wait_for(row_in.at[pl.ds(0, 3)], row_sems.at[1, 1])
    for p in range(4):
        solved_ref[:, p * quarter : (p + 1) * quarter] = row_in[p, 0:4, :]

    wait_for(row_out.at[pl.ds(0, 3)], row_sems.at[1, 0])
    pair_load.wait_send()
    wait_for(squares_in.at[pl.ds(1, 63)], square_sems.at[2])
    wait_for(blocks, reduce_send.at[ITERS - 1])
    for step in range(ITERS + 1):
        wait_for(blocks, gather_send.at[step])
    wait_for(low.at[0], pair_send)
    wait_for(scores, out_sem)


def body(train_grads, query_grads):
    rows, width = train_grads.shape
    quarter = width // 4
    vmem, anywhere = pl.BlockSpec(memory_space=pltpu.VMEM), pl.BlockSpec(memory_space=pl.ANY)
    dma = pltpu.SemaphoreType.DMA
    return pl.pallas_call(
        kernel,
        out_shape=(
            jax.ShapeDtypeStruct((rows, 512), F32),
            jax.ShapeDtypeStruct((4, width), F32),
        ),
        in_specs=[anywhere, vmem],
        out_specs=(anywhere, vmem),
        scratch_shapes=[
            pltpu.VMEM((2 * rows, width), BF16),
            pltpu.VMEM((ITERS, 4, 256, quarter), BF16),
            pltpu.VMEM((4, 512, quarter), BF16),
            pltpu.VMEM((256, 2 * rows), F32),
            pltpu.VMEM((256, 2 * rows), BF16),
            pltpu.VMEM((4, 256, quarter), BF16),
            pltpu.VMEM((ITERS, 64, 16, quarter), BF16),
            pltpu.VMEM((rows, 512), F32),
            pltpu.VMEM((4, 8, quarter), F32),
            pltpu.VMEM((4, 8, quarter), F32),
            pltpu.VMEM((16, quarter), F32),
            pltpu.VMEM((16, quarter), F32),
            pltpu.VMEM((8, 128), F32),
            pltpu.VMEM((2, 1, 128), F32),
            pltpu.VMEM((64, 1, 128), F32),
            dma((3,)),
            dma((2, 2)),
            dma((ITERS + 1,)),
            dma((ITERS + 1, 4)),
            dma,
            dma((4,)),
            dma((ITERS,)),
            dma((ITERS, 4)),
            dma((4,)),
            dma,
        ],
        compiler_params=pltpu.CompilerParams(
            collective_id=0, has_side_effects=True, vmem_limit_bytes=56 * 2**20
        ),
        cost_estimate=pl.CostEstimate(
            flops=10 * rows * width * 512, bytes_accessed=4 * rows * width, transcendentals=0
        ),
    )(train_grads, query_grads)


def solution(mesh):
    placed = (P(("train", "query"), None), P(("train", "query"), None))
    return jax.shard_map(
        body,
        mesh=mesh,
        in_specs=placed,
        out_specs=placed,
        check_vma=False,
    )
```

time: 1290 us -> 119 us (0.09)
  waiting for transfers between devices: 1140 us -> 0 us
  Pallas kernels: 0 us -> 113 us
  blocking collectives: 66.3 us -> 0 us
  matrix products: 42.8 us -> 0 us
  between operations: 14.5 us -> 0.65 us
    all_gather x3 -> x0, waiting for transfers between devices: 908 us -> none  [project(): lax.all_gather(low_state, ('train', 'query'), axis=0, tiled=True)]
    unnamed x7 -> x0, waiting for transfers between devices: 234 us -> none
    pallas_call x0 -> x1, Pallas kernels: none -> 113 us  [body(): pl.pallas_call(kernel, out_shape=(jax.ShapeDtypeStruct((rows, 512), F32),...]
    psum x1 -> x0, blocking collectives: 66.3 us -> none  [body(): total = lax.psum(own_sum, ('train', 'query'))]
    dot_general x3 -> x0, matrix products: 42.8 us -> none  [the longest x2 33.4 us: body(): lax.dot_general(inner, train_grads, (((0,), (0,)), ((), ())), preferred_e...]
  transfers between devices with their start and end apart: 5 -> 0, of which waited for: 5 -> 0; matrix products, arithmetic and copies ran while one was open for 1% -> 0% of each run, Pallas kernels for 0% -> 0%
where the time goes in v1:
time: 119 us
  Pallas kernels  113 us (95%)
  local copies, waits for them, and re-layouts  5.26 us (4%)
    pallas_call x1, Pallas kernels, body(): pl.pallas_call(kernel, out_shape=(jax.ShapeDtypeStruct((rows, 512), F32),...  113 us
    unnamed x4, local copies, waits for them, and re-layouts  5.26 us

profile of v1, /device:TPU:1, one launch (start us, length us, event | category | flops | bytes accessed | tf_op | source)
XLA Modules:
  0.0 119.0 jit_solution(10720852836919942208)
XLA Ops:
  0.6 113.1 %shard_map.41 = (f32[2048,512]{1,0:T(8,128)}, f32[4,2048]{1,0:T(4,128)}) custom-call(bf16[2048,2048]{1,0:T(8,128)(2,1)} %grads_ref.1, bf16[4,2048]{1,0:T(4,128)(2,1)} %query_ref.1), custom_call_target="tpu_custom_call" | custom-call | flops 21474836480 | bytes 16777216 | tf_op jit(solution)/shard_map/pallas_call | solution.py:273
  113.8 0.0 copy-start
  113.8 4.6 %copy.6 = f32[2048,512]{1,0:T(8,128)} copy(f32[2048,512]{1,0:T(8,128)} %get-tuple-element.4) | data formatting | bytes 8388608
  118.4 0.0 copy-done
  118.4 0.6 copy.7
Async XLA Ops:
  113.8 4.7 %copy-start = (f32[4,2048]{1,0:T(4,128)S(1)}, f32[4,2048]{1,0:T(4,128)}, u32[]{:S(2)}) copy-start(f32[4,2048]{1,0:T(4,128)} %get-tuple-element.5) | copy-start | bytes 98308

commit v2 on v1

--- a/solution.py
+++ b/solution.py
@@ -10,8 +10,8 @@
 ITERS = 2
 MESH = pl.DeviceIdType.MESH
 F32, BF16 = jnp.float32, jnp.bfloat16
-ORDER = (0, 1, 3, 2)
-TILE = 512
+ORDER = (1, 2, 3, 0)
+AHEAD = 4
 
 
 def div(a, b):
@@ -30,20 +30,23 @@
     return lax.dot_general(a, b, (((1,), (0,)), ((), ())), preferred_element_type=F32)
 
 
+def far(i):
+    return rem(2 + div(i * (i + 1), 2), 4)
+
+
 def wait_for(ref, sem):
     pltpu.make_async_copy(ref, ref, sem).wait()
 
 
 def kernel(
     grads_ref, query_ref, scores_ref, solved_ref,
-    grads, low, low_all, acc, inner, outgoing, arrived, scores,
+    grads, low, low_all, acc, inner, outgoing, arrived,
     row_out, row_in, query, state, squares, square_out, squares_in,
     grads_sems, row_sems, gather_send, gather_recv, pair_send, pair_recv,
-    reduce_send, reduce_recv, square_sems, out_sem,
+    reduce_send, reduce_recv, square_sems,
 ):
     rows, width = grads_ref.shape
     quarter = width // 4
-    half = low.shape[2]
     train, along = lax.axis_index("train"), lax.axis_index("query")
     core, x, y_hi = rem(train, 2), rem(div(train, 2), 4), div(train, 8)
     y_lo, z = div(along, 4), rem(along, 4)
@@ -52,11 +55,13 @@
     def group_of(px, py):
         return (div(py, 2) * 4 + px) * 2 + rem(py, 2)
 
-    def peer(at, dz):
-        px, py, pz = rem(x + div(at, 4), 4), rem(y + rem(at, 4), 4), rem(z + dz, 4)
+    def peer(at, dist):
+        dx, dy = div(at, 4), rem(at, 4)
+        px, py, pz = rem(x + dx, 4), rem(y + dy, 4), rem(z + dist + 8 - dx - dy, 4)
         return (div(py, 2) * 8 + px * 2 + core, rem(py, 2) * 4 + pz), group_of(px, py)
 
     blocks = arrived.at[0, pl.ds(1, 63)]
+    spot = rem(x + y + z, 4)
     sibling = (train + 1 - 2 * core, along)
     mine = group_of(x, y)
     mine_at = pl.multiple_of(mine * 16, 16)
@@ -84,13 +89,13 @@
         row_out[p, 0:4, :] = query_ref[:, p * quarter : (p + 1) * quarter].astype(F32)
     pl.semaphore_wait(barrier, 64)
 
-    def exchange_rows(sems):
+    def exchange_rows(first, slot, sems):
         for dz in range(1, 4):
             to, _ = peer(jnp.int32(0), dz)
-            remote(row_out.at[rem(z + dz, 4)], row_in.at[z], sems.at[0], sems.at[1], to).start()
-        row_in[z] = row_out[z]
-
-    exchange_rows(row_sems.at[0])
+            remote(row_out.at[rem(first + dz, 4)], row_in.at[slot], sems.at[0], sems.at[1], to).start()
+        row_in[slot] = row_out[first]
+
+    exchange_rows(spot, z, row_sems.at[0])
     pair_load = remote(grads_ref, grads.at[pl.ds(rows, rows)], grads_sems.at[1], grads_sems.at[2], sibling)
     pair_load.start()
     wait_for(row_in.at[pl.ds(0, 3)], row_sems.at[0, 1])
@@ -99,53 +104,63 @@
     state[...] = query[...]
     wait_for(row_out.at[pl.ds(0, 3)], row_sems.at[0, 0])
 
+    def send_group(step, k, buffer, at):
+        block = buffer.at[spot, pl.ds(at, 16)]
+
+        def send(n, carry):
+            to, _ = peer(far(div(n, 4)) * 4 + far(rem(n, 4)), ORDER[k])
+            remote(block, block, gather_send.at[step, k], gather_recv.at[step, k], to).start()
+            return carry
+
+        lax.fori_loop(0, 15 if ORDER[k] == 0 else 16, send, 0)
+
     def gather(step, buffer, at):
-        buffer[z, pl.ds(at, 16), :] = state[...].astype(BF16)
-        block = buffer.at[z, pl.ds(at, 16)]
-        for dz in ORDER:
-            def send(n, carry, dz=dz):
-                to, _ = peer(n, dz)
-                remote(block, block, gather_send.at[step], gather_recv.at[step, dz], to).start()
-                return carry
-
-            lax.fori_loop(1 if dz == 0 else 0, 16, send, 0)
-
-    def await_group(step, dz):
-        taken = low.at[0, 0]
-        wait_for(taken.at[pl.ds(0, 240)] if dz == 0 else taken, gather_recv.at[step, dz])
-
-    def project(step, k, first, last):
-        p = rem(z + 4 - ORDER[k], 4)
+        buffer[spot, pl.ds(at, 16), :] = state[...].astype(BF16)
+        for k in range(AHEAD):
+            send_group(step, k, buffer, at)
+
+    def group_bytes(k):
+        whole = low.at[0, 0]
+        return whole.at[pl.ds(0, 240)] if ORDER[k] == 0 else whole
+
+    def await_group(step, k, buffer, at):
+        if k + AHEAD < 4:
+            wait_for(group_bytes(k), gather_send.at[step, k])
+            send_group(step, k + AHEAD, buffer, at)
+        wait_for(group_bytes(k), gather_recv.at[step, k])
+
+    def project(step, k):
+        p = rem(spot + 4 - ORDER[k], 4)
         columns = pl.ds(pl.multiple_of(p * quarter, quarter), quarter)
-
-        @pl.loop(first // TILE, last // TILE)
-        def _(i):
-            here = pl.ds(pl.multiple_of(i * TILE, TILE), TILE)
-            part = nt(low[step, p], grads[here, columns])
+        for part in range(2):
+            here = slice(part * rows, (part + 1) * rows)
+            value = nt(low[step, p], grads[here, columns])
             if k == 0:
-                acc[:, here] = part
+                acc[:, here] = value
             elif k < 3:
-                acc[:, here] += part
+                acc[:, here] += value
             else:
-                inner[:, here] = (acc[:, here] + part).astype(BF16)
+                inner[:, here] = (acc[:, here] + value).astype(BF16)
 
     def reduce(step):
         @pl.loop(0, 4)
         def _(j):
-            dz = rem(j + 1, 4)
-            p = rem(z + dz, 4)
+            dist = rem(j + 1, 4)
+            p = rem(spot + dist, 4)
             columns = pl.ds(pl.multiple_of(p * quarter, quarter), quarter)
             outgoing[j] = nn(inner[...], grads[:, columns]).astype(BF16)
 
-            def send(n, carry):
-                @pl.when(n + dz > 0)
+            def send(i, carry):
+                n = far(div(i, 4)) * 4 + far(rem(i, 4))
+
+                @pl.when(n + dist > 0)
                 def _():
-                    to, group = peer(n, dz)
+                    to, group = peer(n, dist)
                     remote(
                         outgoing.at[j, pl.ds(pl.multiple_of(group * 16, 16), 16)],
-                        arrived.at[step, dz * 16 + n],
+                        arrived.at[step, dist * 16 + n],
                         reduce_send.at[step],
-                        reduce_recv.at[step, dz],
+                        reduce_recv.at[step, dist],
                         to,
                     ).start()
 
@@ -157,9 +172,9 @@
             return lax.fori_loop(first, last, lambda n, t: t + arrived[step, n].astype(F32), total)
 
         total = outgoing[3, pl.ds(mine_at, 16), :].astype(F32)
-        for dz in (1, 2, 3):
-            wait_for(arrived.at[step, pl.ds(dz * 16, 16)], reduce_recv.at[step, dz])
-            total = add(dz * 16, dz * 16 + 16, total)
+        for dist in (1, 2, 3):
+            wait_for(arrived.at[step, pl.ds(dist * 16, 16)], reduce_recv.at[step, dist])
+            total = add(dist * 16, dist * 16 + 16, total)
         wait_for(arrived.at[step, pl.ds(1, 15)], reduce_recv.at[step, 0])
         return add(1, 16, total)
 
@@ -189,19 +204,14 @@
 
     lax.fori_loop(1, 64, send_squares, 0)
 
-    for k in range(4):
-        await_group(0, ORDER[k])
-        project(0, k, 0, rows)
     pair_load.wait_recv()
-    for k in range(4):
-        project(0, k, rows, 2 * rows)
 
     coef = None
     for step in range(ITERS):
+        for k in range(4):
+            await_group(step, k, low.at[step], mine_at)
+            project(step, k)
         if step > 0:
-            for k in range(4):
-                await_group(step, ORDER[k])
-                project(step, k, 0, 2 * rows)
             wait_for(blocks, reduce_send.at[step - 1])
         curve = reduce(step)
         if step == 0:
@@ -215,31 +225,27 @@
 
     for p in range(4):
         row_out[p, 0:4, :] = state[p * 4 : p * 4 + 4, :]
-    exchange_rows(row_sems.at[1])
+    exchange_rows(z, spot, row_sems.at[1])
 
     def strip_of(p, m):
         return low_all.at[p, pl.ds(pl.multiple_of(m * 64 + core * 32, 32), 32)]
 
     def score(k):
-        p = rem(z + 4 - ORDER[k], 4)
+        p = rem(spot + 4 - ORDER[k], 4)
         columns = pl.ds(pl.multiple_of(p * quarter, quarter), quarter)
 
-        @pl.loop(0, rows // TILE)
-        def _(i):
-            here = pl.ds(pl.multiple_of(i * TILE, TILE), TILE)
-            part = nt(grads[here, columns], low_all[p])
-            if k == 0:
-                scores[here, :] = part
-            elif k < 3:
-                scores[here, :] += part
-            else:
-                scores[here, :] = (scores[here, :] + part) * (1.0 / width**0.5)
-                pltpu.make_async_copy(scores.at[here], scores_ref.at[here], out_sem).start()
+        part = nt(grads[0:rows, columns], low_all[p])
+        if k == 0:
+            scores_ref[...] = part
+        elif k < 3:
+            scores_ref[...] += part
+        else:
+            scores_ref[...] = (scores_ref[...] + part) * (1.0 / width**0.5)
 
     for k in range(5):
         if k < 4:
-            await_group(ITERS, ORDER[k])
-            p = rem(z + 4 - ORDER[k], 4)
+            await_group(ITERS, k, low_all, all_at)
+            p = rem(spot + 4 - ORDER[k], 4)
 
             def pass_on(m, carry, p=p, k=k):
                 strip = strip_of(p, m)
@@ -260,9 +266,9 @@
     wait_for(squares_in.at[pl.ds(1, 63)], square_sems.at[2])
     wait_for(blocks, reduce_send.at[ITERS - 1])
     for step in range(ITERS + 1):
-        wait_for(blocks, gather_send.at[step])
+        for k in range(4 - AHEAD, 4):
+            wait_for(group_bytes(k), gather_send.at[step, k])
     wait_for(low.at[0], pair_send)
-    wait_for(scores, out_sem)
 
 
 def body(train_grads, query_grads):
@@ -277,7 +283,7 @@
             jax.ShapeDtypeStruct((4, width), F32),
         ),
         in_specs=[anywhere, vmem],
-        out_specs=(anywhere, vmem),
+        out_specs=(vmem, vmem),
         scratch_shapes=[
             pltpu.VMEM((2 * rows, width), BF16),
             pltpu.VMEM((ITERS, 4, 256, quarter), BF16),
@@ -286,7 +292,6 @@
             pltpu.VMEM((256, 2 * rows), BF16),
             pltpu.VMEM((4, 256, quarter), BF16),
             pltpu.VMEM((ITERS, 64, 16, quarter), BF16),
-            pltpu.VMEM((rows, 512), F32),
             pltpu.VMEM((4, 8, quarter), F32),
             pltpu.VMEM((4, 8, quarter), F32),
             pltpu.VMEM((16, quarter), F32),
@@ -296,17 +301,16 @@
             pltpu.VMEM((64, 1, 128), F32),
             dma((3,)),
             dma((2, 2)),
-            dma((ITERS + 1,)),
+            dma((ITERS + 1, 4)),
             dma((ITERS + 1, 4)),
             dma,
             dma((4,)),
             dma((ITERS,)),
             dma((ITERS, 4)),
             dma((4,)),
-            dma,
-        ],
+            ],
         compiler_params=pltpu.CompilerParams(
-            collective_id=0, has_side_effects=True, vmem_limit_bytes=56 * 2**20
+            collective_id=0, has_side_effects=True, vmem_limit_bytes=44 * 2**20
         ),
         cost_estimate=pl.CostEstimate(
             flops=10 * rows * width * 512, bytes_accessed=4 * rows * width, transcendentals=0

time: 119 us -> 106 us (0.89)
  Pallas kernels: 113 us -> 102 us
  local copies, waits for them, and re-layouts: 5.26 us -> 3.34 us
    pallas_call x1, Pallas kernels: 113 us -> 102 us  [body(): pl.pallas_call(kernel, out_shape=(jax.ShapeDtypeStruct((rows, 512), F32),...]
    unnamed x4, local copies, waits for them, and re-layouts: 5.26 us -> 3.34 us
where the time goes in v2:
time: 106 us
  Pallas kernels  102 us (96%)
  local copies, waits for them, and re-layouts  3.34 us (3%)
    pallas_call x1, Pallas kernels, body(): pl.pallas_call(kernel, out_shape=(jax.ShapeDtypeStruct((rows, 512), F32),...  102 us
    unnamed x4, local copies, waits for them, and re-layouts  3.34 us

profile of v2, /device:TPU:1, one launch (start us, length us, event | category | flops | bytes accessed | tf_op | source)
XLA Modules:
  0.0 106.3 jit_solution(15686945073686646361)
XLA Ops:
  0.6 0.0 copy-start
  0.6 0.7 copy-done
  1.3 102.3 %shard_map.41 = (f32[2048,512]{1,0:T(8,128)S(1)}, f32[4,2048]{1,0:T(4,128)S(1)}) custom-call(bf16[2048,2048]{1,0:T(8,128)(2,1)} %grads_ref.1, bf16[4,2048]{1,0:T(4,128)(2,1)S(1)} %copy-done), custom_call_target="tpu_custom_call" | custom-call | flops 21474836480 | bytes 16777216 | tf_op jit(solution)/shard_map/pallas_call | solution.py:279
  103.7 2.0 %copy.6 = f32[2048,512]{1,0:T(8,128)} copy(f32[2048,512]{1,0:T(8,128)S(1)} %get-tuple-element.4) | data formatting | bytes 8388608
  105.7 0.6 copy.7
Async XLA Ops:
  0.6 0.7 copy-start

commit v3 on v2

--- a/solution.py
+++ b/solution.py
@@ -87,6 +87,17 @@
     row_out[...] = jnp.zeros_like(row_out)
     for p in range(4):
         row_out[p, 0:4, :] = query_ref[:, p * quarter : (p + 1) * quarter].astype(F32)
+    own_load.wait()
+
+    def square(i, total):
+        strip = pl.ds(pl.multiple_of(i * 256, 256), 256)
+        part = jnp.zeros((256, 128), F32)
+        for j in range(width // 128):
+            value = grads[strip, j * 128 : (j + 1) * 128].astype(F32)
+            part = part + value * value
+        return total + jnp.sum(part.reshape(32, 8, 128), axis=0)
+
+    own = lax.fori_loop(0, rows // 256, square, jnp.zeros((8, 128), F32))
     pl.semaphore_wait(barrier, 64)
 
     def exchange_rows(first, slot, sems):
@@ -143,30 +154,25 @@
                 inner[:, here] = (acc[:, here] + value).astype(BF16)
 
     def reduce(step):
-        @pl.loop(0, 4)
-        def _(j):
-            dist = rem(j + 1, 4)
+        for j in range(4):
+            dist = (j + 1) % 4
             p = rem(spot + dist, 4)
             columns = pl.ds(pl.multiple_of(p * quarter, quarter), quarter)
             outgoing[j] = nn(inner[...], grads[:, columns]).astype(BF16)
 
-            def send(i, carry):
+            def send(i, carry, j=j, dist=dist):
                 n = far(div(i, 4)) * 4 + far(rem(i, 4))
-
-                @pl.when(n + dist > 0)
-                def _():
-                    to, group = peer(n, dist)
-                    remote(
-                        outgoing.at[j, pl.ds(pl.multiple_of(group * 16, 16), 16)],
-                        arrived.at[step, dist * 16 + n],
-                        reduce_send.at[step],
-                        reduce_recv.at[step, dist],
-                        to,
-                    ).start()
-
+                to, group = peer(n, dist)
+                remote(
+                    outgoing.at[j, pl.ds(pl.multiple_of(group * 16, 16), 16)],
+                    arrived.at[step, dist * 16 + n],
+                    reduce_send.at[step],
+                    reduce_recv.at[step, dist],
+                    to,
+                ).start()
                 return carry
 
-            lax.fori_loop(0, 16, send, 0)
+            lax.fori_loop(0, 16 if dist else 15, send, 0)
 
         def add(first, last, total):
             return lax.fori_loop(first, last, lambda n, t: t + arrived[step, n].astype(F32), total)
@@ -180,17 +186,6 @@
 
     gather(0, low.at[0], mine_at)
 
-    own_load.wait()
-
-    def square(i, total):
-        strip = pl.ds(pl.multiple_of(i * 256, 256), 256)
-        part = jnp.zeros((256, 128), F32)
-        for j in range(width // 128):
-            value = grads[strip, j * 128 : (j + 1) * 128].astype(F32)
-            part = part + value * value
-        return total + jnp.sum(part.reshape(32, 8, 128), axis=0)
-
-    own = lax.fori_loop(0, rows // 256, square, jnp.zeros((8, 128), F32))
     square_out[0] = jnp.sum(own, axis=0, keepdims=True)
     to_sibling = remote(square_out.at[0], square_out.at[1], square_sems.at[0], square_sems.at[1], sibling)
     to_sibling.start()

time: 106 us -> 104 us (0.981)
  Pallas kernels: 102 us -> 100 us
    pallas_call x1, Pallas kernels: 102 us -> 100 us  [body(): pl.pallas_call(kernel, out_shape=(jax.ShapeDtypeStruct((rows, 512), F32),...]
where the time goes in v3:
time: 104 us
  Pallas kernels  100 us (96%)
  local copies, waits for them, and re-layouts  3.34 us (3%)
    pallas_call x1, Pallas kernels, body(): pl.pallas_call(kernel, out_shape=(jax.ShapeDtypeStruct((rows, 512), F32),...  100 us
    unnamed x4, local copies, waits for them, and re-layouts  3.34 us

profile of v3, /device:TPU:1, one launch (start us, length us, event | category | flops | bytes accessed | tf_op | source)
XLA Modules:
  0.0 104.1 jit_solution(6041131415045656968)
XLA Ops:
  0.6 0.0 copy-start
  0.6 0.7 copy-done
  1.3 100.1 %shard_map.41 = (f32[2048,512]{1,0:T(8,128)S(1)}, f32[4,2048]{1,0:T(4,128)S(1)}) custom-call(bf16[2048,2048]{1,0:T(8,128)(2,1)} %grads_ref.1, bf16[4,2048]{1,0:T(4,128)(2,1)S(1)} %copy-done), custom_call_target="tpu_custom_call" | custom-call | flops 21474836480 | bytes 16777216 | tf_op jit(solution)/shard_map/pallas_call | solution.py:274
  101.5 2.0 %copy.6 = f32[2048,512]{1,0:T(8,128)} copy(f32[2048,512]{1,0:T(8,128)S(1)} %get-tuple-element.4) | data formatting | bytes 8388608
  103.5 0.6 copy.7
Async XLA Ops:
  0.6 0.7 copy-start
